TPU v7x, 512 devices: a whole 4x4x16 slice. The times are simulated.
512 devices in a mesh: dp: 4 (over y), vocab: 128 (over z, x, core).
Axes of the slice: x: 4, y: 4, z: 16, core: 2. Of those that a mesh axis runs over, the one named last changes fastest.
Arguments:
- hidden: bfloat16 [512, 4096], P('dp'), may hold values from -32 to 32
- head_weight: bfloat16 [4096, 151936], P('dp', 'vocab'), may hold values from -0.5 to 0.5
- frozen_logits: bfloat16 [512, 151936], P('dp', 'vocab'), may hold values from -9 to 15
- frozen_norms: float32 [512], P('dp'), may hold values from 9 to 27, as said below
- advantages: float32 [512], P('dp'), may hold values from -4 to 4
- ratios: float32 [512], P('dp'), may hold values from 0.6 to 1.45
- target_tokens: int32 [512], P('dp'), may hold values from 0 to 151935, as said below
- counted: int32 [512], P('dp'), may hold values from 0 to 1, as said below
Outputs:
- grad_hidden: bfloat16 [512, 4096], P(None, ('dp', 'vocab'))
- grad_head: bfloat16 [4096, 151936], P('dp', 'vocab')
- divergence: float32 [512], P('dp')
Inputs may be any that keep to these rules, and one draw needn't show every extreme that they name: `frozen_norms`: each token's log-sum-exp of frozen_logits over the vocabulary, taken in float32. `target_tokens`: ids of the vocabulary; the last token's target is the end token, id 151936 - 1. 1 marks a counted token; the last token is always counted.
All inputs are finite; a program needn't handle non-finite values.
Results may differ from a plain program's by a relative error of at most 0.0049.
Values may be sent and summed in bfloat16 or wider, within the bound.
A program may use at most 64 MiB of HBM per device.

v0:
```python
import jax
import jax.numpy as jnp
from jax import lax
from jax.sharding import PartitionSpec as P

clip_eps = 0.2
penalty = 0.1


def local(
    hidden, head_weight, frozen_logits, frozen_norms, advantages, ratios, target_tokens, counted
):
    whole_head = lax.all_gather(head_weight, "dp", axis=0, tiled=True)
    logits = jnp.dot(hidden, whole_head, preferred_element_type=jnp.float32)
    frozen = frozen_logits.astype(jnp.float32)
    vocab_here = logits.shape[1]
    row_top = lax.pmax(jnp.max(logits, axis=1), "vocab")
    shifted = jnp.exp(logits - row_top[:, None])
    row_total, row_cross = lax.psum(
        (jnp.sum(shifted, axis=1), jnp.sum(shifted * (logits - frozen), axis=1)), "vocab"
    )
    divergence = row_cross / row_total - row_top - jnp.log(row_total) + frozen_norms
    probabilities = shifted / row_total[:, None]
    mask_values = counted.astype(jnp.float32)
    counted_total = lax.psum(jnp.sum(mask_values), "dp")
    weight = mask_values / counted_total
    active = jnp.where(advantages >= 0.0, ratios <= 1.0 + clip_eps, ratios >= 1.0 - clip_eps)
    policy = jnp.where(active, -advantages * ratios, jnp.zeros_like(ratios))
    vocab_start = lax.axis_index("vocab") * vocab_here
    onehot = (
        target_tokens[:, None] == vocab_start + jnp.arange(vocab_here, dtype=jnp.int32)[None, :]
    ).astype(jnp.float32)
    grad_logits = weight[:, None] * (
        policy[:, None] * (onehot - probabilities)
        + penalty * probabilities * (logits - frozen - (row_cross / row_total)[:, None])
    )
    grad_logits = grad_logits.astype(jnp.bfloat16)
    hidden_cols = lax.all_to_all(hidden, "dp", split_axis=1, concat_axis=0, tiled=True)
    grad_head = lax.dot_general(
        hidden_cols,
        lax.all_gather(grad_logits, "dp", axis=0, tiled=True),
        (((0,), (0,)), ((), ())),
        preferred_element_type=jnp.float32,
    ).astype(jnp.bfloat16)
    partial_value = lax.dot_general(
        grad_logits, whole_head, (((1,), (1,)), ((), ())), preferred_element_type=jnp.float32
    )
    arrived = lax.all_to_all(partial_value, "dp", split_axis=1, concat_axis=0, tiled=True)
    grad_hidden = lax.psum_scatter(arrived, "vocab", scatter_dimension=1, tiled=True).astype(
        jnp.bfloat16
    )
    return (grad_hidden, grad_head, divergence)


def solution(mesh):
    return jax.shard_map(
        local,
        mesh=mesh,
        in_specs=(
            P("dp", None),
            P("dp", "vocab"),
            P("dp", "vocab"),
            P("dp"),
            P("dp"),
            P("dp"),
            P("dp"),
            P("dp"),
        ),
        out_specs=(P(None, ("dp", "vocab")), P("dp", "vocab"), P("dp")),
        check_vma=False,
    )
```

profile of v0, /device:TPU:1, one launch (start us, length us, event | category | flops | bytes accessed | tf_op | source)
XLA Modules:
  0.0 929.4 jit_solution(11396715445117874572)
XLA Ops:
  7.2 0.0 all-gather.3.cloned.1.call-start
  7.2 0.7 all-gather.3.cloned.1.call-update
  7.9 0.0 all-gather.5.cloned.1.call-start
  8.0 0.6 convert_reduce_fusion
  8.6 10.2 %psum.21 = f32[]{:T(128)} all-reduce(f32[]{:T(128)} %convert_reduce_fusion), channel_id=1, replica_groups=mesh['dp'=4,'vocab'=128] {'dp'}, use_global_device_ids=true, to_apply=%region_1.0 | all-reduce | flops 1 | bytes 8 | tf_op jit(solution)/shard_map/psum | solution.py:25
  18.8 0.6 convert_divide_fusion
  19.5 98.4 %all-gather.3.cloned.1.call-done = bf16[4096,1187]{0,1:T(8,128)(2,1)} async-done(((bf16[1024,1187]{0,1:T(8,128)(2,1)}), bf16[4096,1187]{0,1:T(8,128)(2,1)}) %all-gather.3.cloned.1.call-update) | async-done | bytes 9723920 | tf_op jit(solution)/shard_map/all_gather | solution.py:13
  117.9 5.4 fusion.2
  123.3 248.1 %pmax.7 = f32[128]{0:T(128)S(1)} all-reduce(f32[128]{0:T(128)S(1)} %get-tuple-element.9), channel_id=1, replica_groups=mesh['dp'=4,'vocab'=128] {'vocab'}, use_global_device_ids=true, to_apply=%region_3.0 | all-reduce | flops 128 | bytes 1024 | tf_op jit(solution)/shard_map/pmax | solution.py:17
  371.4 0.2 fusion.1
  371.6 251.1 %all-reduce = (f32[128]{0:T(128)S(1)}, f32[128]{0:T(128)S(1)}) all-reduce(f32[128]{0:T(128)S(1)} %get-tuple-element.4, f32[128]{0:T(128)S(1)} %get-tuple-element.3), channel_id=1, replica_groups=mesh['dp'=4,'vocab'=128] {'vocab'}, use_global_device_ids=true, to_apply=%region_7.0 | all-reduce | flops 256 | bytes 2048 | tf_op jit(solution)/shard_map/psum | solution.py:19
  622.7 0.5 subtract_add_fusion
  623.3 1.0 multiply_convert_fusion
  624.3 0.0 reduce-scatter.2.cloned.1.call-start
  624.4 5.6 fusion.3
  630.0 0.1 copy.22
  630.1 37.9 %all_to_all.38 = f32[128,4,1024]{2,0,1:T(8,128)S(1)} all-to-all(f32[128,4,1024]{2,0,1:T(8,128)S(1)} %bitcast.19), channel_id=1, replica_groups=mesh['dp'=4,'vocab'=128] {'dp'}, dimensions={1} | all-to-all | bytes 4194304 | tf_op jit(solution)/shard_map/all_to_all | solution.py:48
  668.0 1.9 copy.17
  669.9 0.7 copy.18
  670.6 14.5 %all_to_all.39 = bf16[128,4,1024]{0,2,1:T(8,128)(2,1)S(1)} all-to-all(bf16[128,4,1024]{0,2,1:T(8,128)(2,1)S(1)} %bitcast.22), channel_id=1, replica_groups=mesh['dp'=4,'vocab'=128] {'dp'}, dimensions={1} | all-to-all | bytes 2097152 | tf_op jit(solution)/shard_map/all_to_all | solution.py:38
  685.1 0.5 copy.19
  685.7 4.2 fusion
  689.8 231.7 %reduce-scatter.2.cloned.1.call-done = f32[512,8]{0,1:T(8,128)} async-done(((f32[512,1024]{0,1:T(8,128)}), f32[512,8]{0,1:T(8,128)}) %reduce-scatter.2.cloned.1.call-update) | async-done | bytes 16400 | tf_op jit(solution)/shard_map/reduce_scatter | solution.py:49
  921.5 1.3 convert_element_type.25
  (19 shorter events, 0.1 us)
Async XLA Ops:
  7.2 0.8 copy-start.4
  7.2 12.2 %copy-start.5 = (f32[128]{0:T(128)S(1)}, f32[128]{0:T(128)}, u32[]{:S(2)}) copy-start(f32[128]{0:T(128)} %param.13) | copy-start | bytes 1540
  7.2 12.2 %copy-start.6 = (f32[128]{0:T(128)S(1)}, f32[128]{0:T(128)}, u32[]{:S(2)}) copy-start(f32[128]{0:T(128)} %param.12) | copy-start | bytes 1540
  7.2 110.7 %copy-start = (bf16[128,4096]{1,0:T(8,128)(2,1)S(1)}, bf16[128,4096]{1,0:T(8,128)(2,1)}, u32[]{:S(2)}) copy-start(bf16[128,4096]{1,0:T(8,128)(2,1)} %param.8) | copy-start | bytes 3145732
  7.2 110.7 %all-gather.3.cloned.1.call-start = ((), (), s32[]{:S(2)}) async-start(), calls=%async_computation.3 | async-start | bytes 12206080 | tf_op jit(solution)/shard_map/all_gather | solution.py:13
  7.9 677.7 %all-gather.5.cloned.1.call-start = ((), (), s32[]{:S(2)}) async-start(), calls=%async_computation.5 | async-start | bytes 1525760 | tf_op jit(solution)/shard_map/all_gather | solution.py:41
  19.4 352.0 %copy-start.1 = (bf16[128,1187]{0,1:T(8,128)(2,1)S(1)}, bf16[128,1187]{0,1:T(8,128)(2,1)}, u32[]{:S(2)}) copy-start(bf16[128,1187]{0,1:T(8,128)(2,1)} %param.10) | copy-start | bytes 911620
  19.5 603.3 %copy-start.3 = (f32[128]{0:T(128)S(1)}, f32[128]{0:T(128)}, u32[]{:S(2)}) copy-start(f32[128]{0:T(128)} %param.11) | copy-start | bytes 1540
  19.5 603.8 %copy-start.2 = (s32[128]{0:T(128)S(1)}, s32[128]{0:T(128)}, u32[]{:S(2)}) copy-start(s32[128]{0:T(128)} %param.14) | copy-start | bytes 1540
  624.3 297.2 %reduce-scatter.2.cloned.1.call-start = ((), (), s32[]{:S(2)}) async-start(), calls=%async_computation.4 | async-start | bytes 2113536 | tf_op jit(solution)/shard_map/reduce_scatter | solution.py:49
Sparse Core Ops, SparseCore 0:
  10.1 107.6 all-gather.2
  624.5 45.1 all-gather.4
  674.2 247.2 reduce-scatter.1
where the time goes:
time: 940 us; the launch traced here: 929 us
  blocking collectives  562 us (60%)
  waiting for transfers between devices  331 us (35%)
  matrix products  15.1 us (2%)
  between operations  13.9 us (1%)
    psum x1, blocking collectives, local(): lax.psum((jnp.sum(shifted, axis=1), jnp.sum(shifted * (logits - frozen),...  251 us
    pmax x1, blocking collectives, local(): row_top = lax.pmax(jnp.max(logits, axis=1), 'vocab')  248 us
    reduce_scatter x1, waiting for transfers between devices, local(): lax.psum_scatter(arrived, 'vocab', scatter_dimension=1, tiled=True)  232 us
    all_gather x1, waiting for transfers between devices, local(): whole_head = lax.all_gather(head_weight, 'dp', axis=0, tiled=True)  98.4 us
    all_to_all x1, blocking collectives, local(): lax.all_to_all(partial_value, 'dp', split_axis=1, concat_axis=0, tiled=True)  37.9 us
  transfers between devices with their start and end apart: 3, of which 2 were waited for; matrix products, arithmetic and copies ran while one was open for 2% of the time, Pallas kernels for 0%

commit v1 on v0

v1 whole, which is shorter than its diff:
```python
import functools

import jax
import jax.numpy as jnp
from jax import lax
from jax.experimental import pallas as pl
from jax.experimental.pallas import tpu as pltpu
from jax.sharding import PartitionSpec as P

clip_eps = 0.2
penalty = 0.1

NX = 4
HALF = 608
PIECES = ((0, 320), (320, 288))
SENT = (608, 592)
ROWS = 2 * HALF
DEEP = 1280
ONE = 512.0
TWO = 256.0
MESH = pl.DeviceIdType.MESH
F32 = jnp.float32
BF16 = jnp.bfloat16


def pack(values, scale):
    top = 8388607.0
    whole = jnp.clip(jnp.floor(values * scale + 0.5), -top, top).astype(jnp.int32)
    quarter = values.shape[0] // 4
    a, b, c, d = (whole[k * quarter : (k + 1) * quarter] for k in range(4))
    low = 0xFFFFFF
    return (
        (a & low) | (d << 24),
        (b & low) | ((d >> 8) << 24),
        (c & low) | ((d >> 16) << 24),
    )


def unpack(u, v, w, scale):
    parts = [(word << 8) >> 8 for word in (u, v, w)]
    parts.append(((u >> 24) & 0xFF) | (((v >> 24) & 0xFF) << 8) | ((w >> 24) << 16))
    back = 1.0 / scale
    return [part.astype(F32) * back for part in parts]


def kernel(
    devices,
    hidden, head, frozen, norms, advantages, ratios, targets, counted,
    out_hidden, out_head, out_div,
    head_v, head_t, tail, frozen_v, frozen_f, hid, via, logits, hold,
    snd2, snd1, snd3, rcv2, rcv1, rcv3,
    cnt, cnt_in, st1, st1_in, st2, st2_in,
    g, prod, prod_in, mid, xs, xs_in, zs, zs_in, total_h, head_o,
    load_sem, h_send, h_recv, sh_send, sh_recv, r_send, r_recv,
    c_send, c_recv, s1_send, s1_recv, s2_send, s2_recv,
    g_send, g_recv, a_send, a_recv, x_send, x_recv, z_send, z_recv, o_sem,
):
    NZ = devices // (2 * NX)
    GROUP = 2 * NX
    width = hid.shape[2]
    vocab_here = head.shape[0]
    me = lax.axis_index("dp")
    v = lax.axis_index("vocab")
    core = lax.rem(v, 2)
    x = lax.rem(v // 2, NX)
    z = v // GROUP
    xc = lax.rem(v, GROUP)
    right, far, left = (lax.rem(me + k, 4) for k in (1, 2, 3))
    sibling = (me, v + 1 - 2 * core)

    def in_group(k):
        return (me, z * GROUP + lax.rem(xc + k, GROUP))

    def along_x(k):
        return (me, z * GROUP + lax.rem(x + k, NX) * 2 + core)

    def along_z(k):
        return (me, lax.rem(z + k, NZ) * GROUP + xc)

    def remote(src, dst, send, recv, device):
        return pltpu.make_async_remote_copy(
            src_ref=src, dst_ref=dst, send_sem=send, recv_sem=recv,
            device_id=device, device_id_type=MESH,
        )

    def lanes(block):
        return pl.ds(pl.multiple_of(block * width, width), width)

    half_tok = hid.shape[1] // 2
    mine = pl.ds(pl.multiple_of(core * half_tok, half_tok), half_tok)

    load_head = pltpu.make_async_copy(head, head_v, load_sem.at[0])
    load_own = pltpu.make_async_copy(hidden.at[:, lanes(me)], hid.at[0], load_sem.at[1])
    load_frozen = pltpu.make_async_copy(frozen, frozen_v, load_sem.at[2])
    barrier = pltpu.get_barrier_semaphore()
    for k in (1, 2, 3):
        pl.semaphore_signal(barrier, inc=1, device_id=(lax.rem(me + k, 4), v), device_id_type=MESH)
    for k in range(1, GROUP):
        pl.semaphore_signal(barrier, inc=1, device_id=in_group(k), device_id_type=MESH)

    def greet(k, carry):
        pl.semaphore_signal(barrier, inc=1, device_id=along_z(k), device_id_type=MESH)
        return carry

    lax.fori_loop(1, NZ, greet, 0)
    load_head.start()
    load_own.start()
    load_frozen.start()
    cnt[...] = counted[...].astype(F32)
    pl.semaphore_wait(barrier, 3 + (GROUP - 1) + (NZ - 1))

    onward = (lax.rem(me + 1 + 2 * core, 4), v)
    h_right = remote(hidden.at[mine, lanes(right)], hid.at[3, mine], h_send.at[0], h_recv.at[0], (right, v))
    h_left = remote(hidden.at[mine, lanes(left)], hid.at[1, mine], h_send.at[1], h_recv.at[1], (left, v))
    h_far = remote(hidden.at[mine, lanes(far)], via, h_send.at[2], h_recv.at[2], onward)
    h_on = remote(via, hid.at[2, mine], h_send.at[3], h_recv.at[3], onward)
    h_right.start()
    h_left.start()
    h_far.start()
    counts = [
        remote(cnt, cnt_in.at[k - 1], c_send.at[k - 1], c_recv.at[k - 1], (lax.rem(me + k, 4), v))
        for k in (1, 2, 3)
    ]
    for copy in counts:
        copy.start()
    share = {
        r: remote(hid.at[r, mine], hid.at[r, mine], sh_send.at[r], sh_recv.at[r], sibling)
        for r in (1, 2, 3)
    }

    for r in range(4):
        g[r, pl.ds(1184, DEEP - 1184)] = jnp.zeros((DEEP - 1184, g.shape[2]), BF16)
    load_head.wait()

    def product(r, start, size):
        valid = min(size, vocab_here - start)
        rows = head_v[pl.ds(start, valid)]
        return valid, lax.dot_general(
            rows, hid[r], (((1,), (1,)), ((), ())), preferred_element_type=F32
        )

    def put(dst, at, r, start, size):
        valid, value = product(r, start, size)
        if valid < size:
            floor = valid // 8 * 8
            dst[pl.ds(at + floor, size - floor)] = jnp.zeros((size - floor, value.shape[1]), F32)
        dst[pl.ds(at, valid)] = value

    def send_packed(buffer, slot, piece, values, scale):
        at, size = PIECES[piece]
        quarter, at = size // 4, at // 4 * 3
        for k, words in enumerate(pack(values, scale)):
            buffer[slot, pl.ds(at + k * quarter, quarter)] = words

    def read_packed(buffer, slot, piece, scale):
        at, size = PIECES[piece]
        quarter, at = size // 4, at // 4 * 3
        return unpack(*(buffer[slot, pl.ds(at + k * quarter, quarter)] for k in range(3)), scale)

    def packed_copy(step, slot, piece):
        snd, rcv = ((snd2, rcv2), (snd1, rcv1), (snd3, rcv3))[step]
        at, size = PIECES[piece]
        rows = pl.ds(at // 4 * 3, size // 4 * 3)
        sem = (step * 2 + slot) * 2 + piece
        return remote(
            snd.at[slot, rows], rcv.at[slot, rows], r_send.at[sem], r_recv.at[sem],
            ((right, left)[slot], v),
        )

    h_left.wait_recv()
    share[1].start()
    h_right.wait_recv()
    share[3].start()

    block = min(128, width)
    whole_blocks = vocab_here // 128
    tail[...] = jnp.zeros_like(tail)
    tail[pl.ds(0, vocab_here - whole_blocks * 128)] = head_v[pl.ds(whole_blocks * 128, vocab_here - whole_blocks * 128)]

    h_far.wait_recv()
    h_on.start()

    share[1].wait_recv()
    for piece, (at, size) in enumerate(PIECES):
        put(hold.at[0], at, 1, HALF + at, size)
        send_packed(snd2, 0, piece, hold[0, pl.ds(at, size)], ONE)
        packed_copy(0, 0, piece).start()
    share[3].wait_recv()
    for piece, (at, size) in enumerate(PIECES):
        put(hold.at[1], at, 3, at, size)
        send_packed(snd2, 1, piece, hold[1, pl.ds(at, size)], ONE)
        packed_copy(0, 1, piece).start()

    h_on.wait_recv()
    share[2].start()
    share[2].wait_recv()
    for piece, (at, size) in enumerate(PIECES):
        put(hold.at[0], at, 2, at, size)
        send_packed(snd1, 0, piece, hold[0, pl.ds(at, size)], ONE)
        packed_copy(1, 0, piece).start()
        put(hold.at[1], at, 2, HALF + at, size)
        send_packed(snd1, 1, piece, hold[1, pl.ds(at, size)], ONE)
        packed_copy(1, 1, piece).start()

    for at, size in PIECES:
        put(hold.at[0], at, 1, at, size)
        put(hold.at[1], at, 3, HALF + at, size)
    load_own.wait()
    for half in (0, HALF):
        for at, size in PIECES:
            put(logits, half + at, 0, half + at, size)

    def turn(j, carry):
        cols = pl.ds(pl.multiple_of(j * block, block), block)
        for i in range(whole_blocks):
            head_t[cols, pl.ds(i * 128, 128)] = head_v[pl.ds(i * 128, 128), cols].T
        head_t[cols, pl.ds(whole_blocks * 128, 128)] = tail[:, cols].T
        return carry

    lax.fori_loop(0, width // block, turn, 0)
    load_frozen.wait()
    frozen_f[pl.ds(1184, ROWS - 1184)] = jnp.zeros((ROWS - 1184, frozen_f.shape[1]), F32)
    frozen_f[pl.ds(0, vocab_here)] = frozen_v[...].astype(F32)

    def add_into(dst, at, piece, parts):
        quarter = PIECES[piece][1] // 4
        for k, part in enumerate(parts):
            rows = pl.ds(at + k * quarter, quarter)
            dst[rows] = dst[rows] + part

    for piece, (at, size) in enumerate(PIECES):
        for slot in (0, 1):
            packed_copy(1, slot, piece).wait_recv()
            add_into(hold.at[slot], at, piece, read_packed(rcv1, slot, piece, ONE))
            send_packed(snd3, slot, piece, hold[slot, pl.ds(at, size)], TWO)
            packed_copy(2, slot, piece).start()

    for slot in (0, 1):
        half = (HALF, 0)[slot]
        for piece, (at, size) in enumerate(PIECES):
            packed_copy(0, slot, piece).wait_recv()
            add_into(logits, half + at, piece, read_packed(rcv2, slot, piece, ONE))
    for piece, (at, size) in enumerate(PIECES):
        for slot in (0, 1):
            half = (0, HALF)[slot]
            packed_copy(2, slot, piece).wait_recv()
            add_into(logits, half + at, piece, read_packed(rcv3, slot, piece, TWO))

    edge = vocab_here // 8 * 8
    rows = edge + lax.broadcasted_iota(jnp.int32, (ROWS - edge, logits.shape[1]), 0)
    logits[pl.ds(edge, ROWS - edge)] = jnp.where(
        rows < vocab_here, logits[pl.ds(edge, ROWS - edge)], -1e30
    )

    step = ROWS // 4
    tops = [jnp.max(logits[pl.ds(k * step, step)], axis=0, keepdims=True) for k in range(4)]
    top = functools.reduce(jnp.maximum, tops)
    total = jnp.zeros_like(top)
    cross = jnp.zeros_like(top)
    for k in range(4):
        piece = pl.ds(k * step, step)
        shifted = jnp.exp(logits[piece] - top)
        total += jnp.sum(shifted, axis=0, keepdims=True)
        cross += jnp.sum(shifted * (logits[piece] - frozen_f[piece]), axis=0, keepdims=True)

    def exchange(top, total, cross, out, into, send, recv, to, count):
        out[0:1] = top
        out[1:2] = total
        out[2:3] = cross
        out[3:4] = cross

        def go(k, carry):
            remote(out, into.at[k], send.at[k], recv.at[k], to(k)).start()
            return carry

        def arrive(k, carry):
            remote(out, into.at[k], send.at[k], recv.at[k], to(k)).wait()
            return carry

        lax.fori_loop(1, count, go, 0)
        lax.fori_loop(1, count, arrive, 0)
        best = top
        for k in range(1, count):
            best = jnp.maximum(best, into[k, 0:1])
        scale = jnp.exp(top - best)
        all_total, all_cross = total * scale, cross * scale
        for k in range(1, count):
            scale = jnp.exp(into[k, 0:1] - best)
            all_total += into[k, 1:2] * scale
            all_cross += into[k, 2:3] * scale
        return best, all_total, all_cross

    top, total, cross = exchange(
        top, total, cross, st1, st1_in, s1_send, s1_recv, in_group, GROUP
    )
    top, total, cross = exchange(top, total, cross, st2, st2_in, s2_send, s2_recv, along_z, NZ)
    mean = cross / total
    out_div[...] = mean - top - jnp.log(total) + norms[...]

    for copy in counts:
        copy.wait()
    all_counts = cnt[...] + cnt_in[0] + cnt_in[1] + cnt_in[2]
    weight = cnt[...] / jnp.sum(all_counts, axis=1, keepdims=True)
    adv, ratio = advantages[...], ratios[...]
    active = jnp.where(adv >= 0.0, (ratio <= 1.0 + clip_eps).astype(F32), (ratio >= 1.0 - clip_eps).astype(F32))
    policy = jnp.where(active > 0.5, -adv * ratio, jnp.zeros_like(ratio))
    target = targets[...] - v * vocab_here
    target = jnp.where(target < vocab_here, target, -1)
    inverse = 1.0 / total
    hits = weight * policy

    def gradient_copy(slot, kind):
        device = ((right, left)[slot], v)
        half = (slot, 1 - slot, slot)[kind]
        rows = pl.ds(half * HALF, SENT[half])
        source = ((0, 0, 3), (0, 0, 1))[slot][kind]
        into = ((3, 3, 2), (1, 1, 2))[slot][kind]
        sem = slot * 3 + kind
        return remote(g.at[source, rows], g.at[into, rows], g_send.at[sem], g_recv.at[sem], device)

    for k in range(4):
        piece = pl.ds(k * step, step)
        value = logits[piece]
        chance = jnp.exp(value - top) * inverse
        rows = k * step + lax.broadcasted_iota(jnp.int32, value.shape, 0)
        grad = weight * (penalty * chance * (value - frozen_f[piece] - mean) - policy * chance)
        grad = jnp.where(rows == target, grad + hits, grad)
        g[0, piece] = grad.astype(BF16)
        if k == 1:
            gradient_copy(0, 0).start()
            gradient_copy(1, 1).start()
    gradient_copy(1, 0).start()
    gradient_copy(0, 1).start()

    chunk = width // 4
    units = chunk // 16

    def partial(sources):
        right_side = [g[r] for r in sources]
        right_side = right_side[0] if len(sources) == 1 else jnp.concatenate(right_side, axis=1)

        for i in range(4):
            value = jnp.dot(head_t[pl.ds(i * chunk, chunk)], right_side, preferred_element_type=F32)
            for j, r in enumerate(sources):
                prod[r, pl.ds(i * units, units)] = value[:, j * 128 : (j + 1) * 128].reshape(units, 2, 8, 128)
        for r in sources:
            pair(r).start()

    def pair(r):
        return remote(prod.at[r, :, 1 - core], prod_in.at[r], a_send.at[r], a_recv.at[r], sibling)

    def x_copy(r, k):
        sem = r * NX + k
        return remote(xs.at[r, k], xs_in.at[r, k], x_send.at[sem], x_recv.at[sem], along_x(k))

    def z_copy(r, k):
        sem = r * NZ + k
        return remote(
            zs.at[r, lax.rem(z + k, NZ)], zs_in.at[r, k], z_send.at[sem], z_recv.at[sem], along_z(k)
        )

    def to_x(r):
        pair(r).wait_recv()
        for k in range(NX):
            there = lax.rem(x + k, NX)
            value = mid_sum(r, there)
            if k == 0:
                mid[r] = value
            else:
                xs[r, k] = value.reshape(NZ * 8, 128).astype(BF16)
                x_copy(r, k).start()

    def mid_sum(r, there):
        return jnp.stack(
            [prod[r, zz * NX + there, core] + prod_in[r, zz * NX + there] for zz in range(NZ)]
        )

    def to_z(r):
        value = mid[r]
        for k in range(1, NX):
            x_copy(r, k).wait_recv()
            value = value + xs_in[r, k].astype(F32).reshape(NZ, 8, 128)
        zs[r] = value

        def go(k, carry):
            z_copy(r, k).start()
            return carry

        lax.fori_loop(1, NZ, go, 0)

    def finish(r):
        def arrive(k, carry):
            z_copy(r, k).wait_recv()
            return carry

        lax.fori_loop(1, NZ, arrive, 0)
        value = zs[r, z]
        for k in range(1, NZ):
            value = value + zs_in[r, k]
        tokens = lax.rem(me + r, 4) * 128
        total_h[:, pl.ds(pl.multiple_of(tokens, 128), 128)] = value

    head_rows = ((0, 304), (304, 304), (608, 304), (912, vocab_here - 912))

    def head_gradient(k):
        at, size = head_rows[k]
        rows = pl.ds(at, size)
        left_side = jnp.concatenate([g[r, rows] for r in range(4)], axis=1)
        tokens = hid[...].reshape(4 * hid.shape[1], width)
        head_o[rows] = jnp.dot(left_side, tokens, preferred_element_type=F32).astype(BF16)
        head_copy(k).start()

    def head_copy(k):
        at, size = head_rows[k]
        return pltpu.make_async_copy(head_o.at[pl.ds(at, size)], out_head.at[pl.ds(at, size)], o_sem.at[k])

    partial((0,))
    to_x(0)
    gradient_copy(0, 0).wait_recv()
    gradient_copy(0, 2).start()
    gradient_copy(1, 0).wait_recv()
    gradient_copy(1, 2).start()
    to_z(0)
    gradient_copy(0, 1).wait_recv()
    gradient_copy(1, 1).wait_recv()
    partial((1, 3))
    to_x(1)
    to_x(3)
    to_z(1)
    to_z(3)
    gradient_copy(0, 2).wait_recv()
    gradient_copy(1, 2).wait_recv()
    partial((2,))
    head_gradient(0)
    to_x(2)
    head_gradient(1)
    head_gradient(2)
    to_z(2)
    head_gradient(3)
    finish(0)
    finish(1)
    finish(3)
    finish(2)
    out_hidden[...] = total_h[...].astype(BF16)

    for copy in (h_right, h_left, h_far, h_on, share[1], share[2], share[3]):
        copy.wait_send()
    for stage in range(3):
        for slot in (0, 1):
            for piece in (0, 1):
                packed_copy(stage, slot, piece).wait_send()
    for slot in (0, 1):
        for kind in range(3):
            gradient_copy(slot, kind).wait_send()
    for r in range(4):
        pair(r).wait_send()
        for k in range(1, NX):
            x_copy(r, k).wait_send()

        def left_z(k, carry):
            z_copy(r, k).wait_send()
            return carry

        lax.fori_loop(1, NZ, left_z, 0)
    for k in range(4):
        head_copy(k).wait()


def local(devices, hidden, head, frozen, norms, advantages, ratios, targets, counted):
    tokens, depth = hidden.shape
    width = depth // 4
    vocab_here = head.shape[1]
    NZ = devices // (2 * NX)
    GROUP = 2 * NX
    units = width // 16
    packed = pltpu.VMEM((2, HALF // 4 * 3, tokens), jnp.int32)
    dma = pltpu.SemaphoreType.DMA
    row = [a.reshape(1, tokens) for a in (norms, advantages, ratios, targets, counted)]
    vmem = pl.BlockSpec(memory_space=pltpu.VMEM)
    anywhere = pl.BlockSpec(memory_space=pl.ANY)
    out = pl.pallas_call(
        functools.partial(kernel, devices),
        out_shape=(
            jax.ShapeDtypeStruct((width // devices, 4 * tokens), BF16),
            jax.ShapeDtypeStruct((vocab_here, width), BF16),
            jax.ShapeDtypeStruct((1, tokens), F32),
        ),
        in_specs=[anywhere] * 3 + [vmem] * 5,
        out_specs=(vmem, anywhere, vmem),
        scratch_shapes=[
            pltpu.VMEM((vocab_here, width), BF16),
            pltpu.VMEM((width, DEEP), BF16),
            pltpu.VMEM((128, width), BF16),
            pltpu.VMEM((vocab_here, tokens), BF16),
            pltpu.VMEM((ROWS, tokens), F32),
            pltpu.VMEM((4, tokens, width), BF16),
            pltpu.VMEM((tokens // 2, width), BF16),
            pltpu.VMEM((ROWS, tokens), F32),
            pltpu.VMEM((2, HALF, tokens), F32),
            packed, packed, packed, packed, packed, packed,
            pltpu.VMEM((1, tokens), F32),
            pltpu.VMEM((3, 1, tokens), F32),
            pltpu.VMEM((4, tokens), F32),
            pltpu.VMEM((GROUP, 4, tokens), F32),
            pltpu.VMEM((4, tokens), F32),
            pltpu.VMEM((NZ, 4, tokens), F32),
            pltpu.VMEM((4, DEEP, tokens), BF16),
            pltpu.VMEM((4, units, 2, 8, tokens), F32),
            pltpu.VMEM((4, units, 8, tokens), F32),
            pltpu.VMEM((4, NZ, 8, tokens), F32),
            pltpu.VMEM((4, NX, NZ * 8, tokens), BF16),
            pltpu.VMEM((4, NX, NZ * 8, tokens), BF16),
            pltpu.VMEM((4, NZ, 8, tokens), F32),
            pltpu.VMEM((4, NZ, 8, tokens), F32),
            pltpu.VMEM((8, 4 * tokens), F32),
            pltpu.VMEM((vocab_here, width), BF16),
            dma((3,)),
            dma((4,)), dma((4,)),
            dma((4,)), dma((4,)),
            dma((12,)), dma((12,)),
            dma((3,)), dma((3,)),
            dma((GROUP,)), dma((GROUP,)),
            dma((NZ,)), dma((NZ,)),
            dma((6,)), dma((6,)),
            dma((4,)), dma((4,)),
            dma((4 * NX,)), dma((4 * NX,)),
            dma((4 * NZ,)), dma((4 * NZ,)),
            dma((4,)),
        ],
        compiler_params=pltpu.CompilerParams(
            collective_id=0, has_side_effects=True, vmem_limit_bytes=48 * 1024 * 1024
        ),
    )(hidden, head.T, frozen.T, *row)
    return out[0].T, out[1].T, out[2].reshape(tokens)


def solution(mesh):
    return jax.shard_map(
        functools.partial(local, mesh.shape["vocab"]),
        mesh=mesh,
        in_specs=(
            P("dp", None),
            P("dp", "vocab"),
            P("dp", "vocab"),
            P("dp"),
            P("dp"),
            P("dp"),
            P("dp"),
            P("dp"),
        ),
        out_specs=(P(None, ("dp", "vocab")), P("dp", "vocab"), P("dp")),
        check_vma=False,
    )
```

time: 940 us -> 96.9 us (0.10); the launches traced: 929 us -> 95.9 us
  blocking collectives: 562 us -> 0 us
  waiting for transfers between devices: 331 us -> 0 us
  Pallas kernels: 0 us -> 87.2 us
  matrix products: 15.1 us -> 0 us
  between operations: 13.9 us -> 0.66 us
    psum x2 -> x0, blocking collectives: 261 us -> none  [the longest x1 251 us: local(): lax.psum((jnp.sum(shifted, axis=1), jnp.sum(shifted * (logits - frozen),...]
    pmax x1 -> x0, blocking collectives: 248 us -> none  [local(): row_top = lax.pmax(jnp.max(logits, axis=1), 'vocab')]
    reduce_scatter x1 -> x0, waiting for transfers between devices: 232 us -> none  [local(): lax.psum_scatter(arrived, 'vocab', scatter_dimension=1, tiled=True)]
    all_gather x2 -> x0, waiting for transfers between devices: 98.4 us -> none  [the longest x1 98.4 us: local(): whole_head = lax.all_gather(head_weight, 'dp', axis=0, tiled=True)]
    pallas_call x0 -> x1, Pallas kernels: none -> 87.2 us  [local(): pl.pallas_call(functools.partial(kernel, devices), out_shape=(jax.ShapeDt...]
    all_to_all x2 -> x0, blocking collectives: 52.4 us -> none  [the longest x1 37.9 us: local(): lax.all_to_all(partial_value, 'dp', split_axis=1, concat_axis=0, tiled=True)]
    dot_general x3 -> x0, matrix products: 15.1 us -> none  [the longest x1 5.58 us: local(): lax.dot_general(grad_logits, whole_head, (((1,), (1,)), ((), ())), prefer...]
  transfers between devices with their start and end apart: 3 -> 0, of which waited for: 2 -> 0; matrix products, arithmetic and copies ran while one was open for 2% -> 0% of each run, Pallas kernels for 0% -> 0%
where the time goes in v1:
time: 96.9 us; the launch traced here: 95.9 us
  Pallas kernels  87.2 us (90%)
  local copies, waits for them, and re-layouts  8 us (8%)
    pallas_call x1, Pallas kernels, local(): pl.pallas_call(functools.partial(kernel, devices), out_shape=(jax.ShapeDt...  87.2 us
    unnamed x17, local copies, waits for them, and re-layouts  8 us

profile of v1, /device:TPU:1, one launch (start us, length us, event | category | flops | bytes accessed | tf_op | source)
XLA Modules:
  0.0 95.9 jit_solution(6868022168295519674)
XLA Ops:
  0.6 0.0 copy-start
  0.6 1.2 %copy-done = bf16[128,4096]{1,0:T(8,128)(2,1)S(1)} copy-done((bf16[128,4096]{1,0:T(8,128)(2,1)S(1)}, bf16[128,4096]{1,0:T(8,128)(2,1)}, u32[]{:S(2)}) %copy-start) | copy-done | bytes 1048600
  1.9 0.0 copy-start.1
  1.9 1.0 %copy-done.1 = bf16[128,1187]{0,1:T(8,128)(2,1)S(1)} copy-done((bf16[128,1187]{0,1:T(8,128)(2,1)S(1)}, bf16[128,1187]{0,1:T(8,128)(2,1)}, u32[]{:S(2)}) %copy-start.1) | copy-done | bytes 303896
  2.8 0.0 copy-start.2
  2.8 0.7 copy-done.2
  3.5 0.0 copy-start.3
  3.5 0.7 copy-done.3
  4.1 0.0 copy-start.4
  4.1 0.7 copy-done.4
  4.8 0.0 copy-start.5
  4.8 0.7 copy-done.5
  5.4 0.0 copy-start.6
  5.5 0.7 copy-done.6
  6.1 87.2 %shard_map.103 = (bf16[8,512]{1,0:T(8,128)(2,1)S(1)}, bf16[1187,1024]{1,0:T(8,128)(2,1)S(1)}, f32[1,128]{1,0:T(1,128)S(1)}) custom-call(bf16[128,4096]{1,0:T(8,128)(2,1)S(1)} %copy-done, bf16[1187,1024]{1,0:T(8,128)(2,1)} %bitcast.19, bf16[1187,128]{1,0:T(8,128)(2,1)S(1)} %bitcast.11, f32[1,128]{1,0:T(1,128)S(1)} %bitcast.13, f32[1,128]{1,0:T(1,128)S(1)} %bitcast.14, ...), custom_call_target="tpu_custom_call" | custom-call | tf_op jit(solution)/shard_map/pallas_call | solution.py:481
  93.4 0.6 copy.14
  94.0 1.4 %copy.15 = bf16[1024,1187]{0,1:T(8,128)(2,1)} copy(bf16[1024,1187]{0,1:T(8,128)(2,1)S(1)} %bitcast.10) | data formatting | bytes 4861952
  95.4 0.5 copy.16
Async XLA Ops:
  0.6 1.2 %copy-start = (bf16[128,4096]{1,0:T(8,128)(2,1)S(1)}, bf16[128,4096]{1,0:T(8,128)(2,1)}, u32[]{:S(2)}) copy-start(bf16[128,4096]{1,0:T(8,128)(2,1)} %hidden.1) | copy-start | bytes 3145732
  1.9 1.0 %copy-start.1 = (bf16[128,1187]{0,1:T(8,128)(2,1)S(1)}, bf16[128,1187]{0,1:T(8,128)(2,1)}, u32[]{:S(2)}) copy-start(bf16[128,1187]{0,1:T(8,128)(2,1)} %param.10) | copy-start | bytes 911620
  2.8 0.7 copy-start.2
  3.5 0.7 copy-start.3
  4.1 0.7 copy-start.4
  4.8 0.7 copy-start.5
  5.4 0.7 copy-start.6

commit v2 on v1

--- a/solution.py
+++ b/solution.py
@@ -45,15 +45,15 @@
 
 def kernel(
     devices,
-    hidden, head, frozen, norms, advantages, ratios, targets, counted,
+    hidden, head, frozen, norms_h, advantages_h, ratios_h, targets_h, counted_h,
     out_hidden, out_head, out_div,
-    head_v, head_t, tail, frozen_v, frozen_f, hid, via, logits, hold,
+    norms, advantages, ratios, targets, counted, head_v, head_t, tail, frozen_v, frozen_f, hid, via, logits, hold,
     snd2, snd1, snd3, rcv2, rcv1, rcv3,
     cnt, cnt_in, st1, st1_in, st2, st2_in,
-    g, prod, prod_in, mid, xs, xs_in, zs, zs_in, total_h, head_o,
+    g, prod, prod_in, mid, xs, xs_in, zs, zs_in, total_h,
     load_sem, h_send, h_recv, sh_send, sh_recv, r_send, r_recv,
     c_send, c_recv, s1_send, s1_recv, s2_send, s2_recv,
-    g_send, g_recv, a_send, a_recv, x_send, x_recv, z_send, z_recv, o_sem,
+    g_send, g_recv, a_send, a_recv, x_send, x_recv, z_send, z_recv, f_sem, hello,
 ):
     NZ = devices // (2 * NX)
     GROUP = 2 * NX
@@ -92,37 +92,56 @@
     load_head = pltpu.make_async_copy(head, head_v, load_sem.at[0])
     load_own = pltpu.make_async_copy(hidden.at[:, lanes(me)], hid.at[0], load_sem.at[1])
     load_frozen = pltpu.make_async_copy(frozen, frozen_v, load_sem.at[2])
-    barrier = pltpu.get_barrier_semaphore()
-    for k in (1, 2, 3):
-        pl.semaphore_signal(barrier, inc=1, device_id=(lax.rem(me + k, 4), v), device_id_type=MESH)
-    for k in range(1, GROUP):
-        pl.semaphore_signal(barrier, inc=1, device_id=in_group(k), device_id_type=MESH)
-
-    def greet(k, carry):
-        pl.semaphore_signal(barrier, inc=1, device_id=along_z(k), device_id_type=MESH)
-        return carry
-
-    lax.fori_loop(1, NZ, greet, 0)
+    load_rows = [
+        pltpu.make_async_copy(src, dst, load_sem.at[3 + k])
+        for k, (src, dst) in enumerate((
+            (counted_h, counted), (norms_h, norms), (advantages_h, advantages),
+            (ratios_h, ratios), (targets_h, targets),
+        ))
+    ]
+    load_rows[0].start()
     load_head.start()
     load_own.start()
     load_frozen.start()
+    for copy in load_rows[1:]:
+        copy.start()
+    barrier = pltpu.get_barrier_semaphore()
+
+    near_y = [(lax.rem(me + k, 4), v) for k in (1, 3)]
+    near_x = [along_x(k) for k in (1, NX - 1)]
+
+    def near_z(k):
+        return [along_z(k), along_z(NZ - k)]
+
+    nearest = [sibling, *near_y, *near_x, *near_z(1)]
+    for device in nearest:
+        pl.semaphore_signal(barrier, inc=1, device_id=device, device_id_type=MESH)
+    rounds = (near_y + near_x + near_z(1), near_x + near_z(2), near_z(4))
+
+    def tell(n):
+        for device in rounds[n]:
+            pl.semaphore_signal(hello.at[n], inc=1, device_id=device, device_id_type=MESH)
+
+    def heard(n):
+        pl.semaphore_wait(hello.at[n], len(rounds[n]))
+
+    load_rows[0].wait()
     cnt[...] = counted[...].astype(F32)
-    pl.semaphore_wait(barrier, 3 + (GROUP - 1) + (NZ - 1))
+    pl.semaphore_wait(barrier, len(nearest))
 
     onward = (lax.rem(me + 1 + 2 * core, 4), v)
     h_right = remote(hidden.at[mine, lanes(right)], hid.at[3, mine], h_send.at[0], h_recv.at[0], (right, v))
     h_left = remote(hidden.at[mine, lanes(left)], hid.at[1, mine], h_send.at[1], h_recv.at[1], (left, v))
     h_far = remote(hidden.at[mine, lanes(far)], via, h_send.at[2], h_recv.at[2], onward)
     h_on = remote(via, hid.at[2, mine], h_send.at[3], h_recv.at[3], onward)
+    h_far.start()
     h_right.start()
     h_left.start()
-    h_far.start()
     counts = [
         remote(cnt, cnt_in.at[k - 1], c_send.at[k - 1], c_recv.at[k - 1], (lax.rem(me + k, 4), v))
         for k in (1, 2, 3)
     ]
-    for copy in counts:
-        copy.start()
+    tell(0)
     share = {
         r: remote(hid.at[r, mine], hid.at[r, mine], sh_send.at[r], sh_recv.at[r], sibling)
         for r in (1, 2, 3)
@@ -130,6 +149,7 @@
 
     for r in range(4):
         g[r, pl.ds(1184, DEEP - 1184)] = jnp.zeros((DEEP - 1184, g.shape[2]), BF16)
+    tail[...] = jnp.zeros_like(tail)
     load_head.wait()
 
     def product(r, start, size):
@@ -167,18 +187,21 @@
             ((right, left)[slot], v),
         )
 
+    h_far.wait_recv()
+    h_on.start()
     h_left.wait_recv()
     share[1].start()
     h_right.wait_recv()
     share[3].start()
 
+    heard(0)
+    tell(1)
+    for copy in counts:
+        copy.start()
+
     block = min(128, width)
     whole_blocks = vocab_here // 128
-    tail[...] = jnp.zeros_like(tail)
     tail[pl.ds(0, vocab_here - whole_blocks * 128)] = head_v[pl.ds(whole_blocks * 128, vocab_here - whole_blocks * 128)]
-
-    h_far.wait_recv()
-    h_on.start()
 
     share[1].wait_recv()
     for piece, (at, size) in enumerate(PIECES):
@@ -191,6 +214,9 @@
         send_packed(snd2, 1, piece, hold[1, pl.ds(at, size)], ONE)
         packed_copy(0, 1, piece).start()
 
+    heard(1)
+    tell(2)
+
     h_on.wait_recv()
     share[2].start()
     share[2].wait_recv()
@@ -219,6 +245,8 @@
 
     lax.fori_loop(0, width // block, turn, 0)
     load_frozen.wait()
+    for copy in load_rows[1:]:
+        copy.wait()
     frozen_f[pl.ds(1184, ROWS - 1184)] = jnp.zeros((ROWS - 1184, frozen_f.shape[1]), F32)
     frozen_f[pl.ds(0, vocab_here)] = frozen_v[...].astype(F32)
 
@@ -234,6 +262,8 @@
             add_into(hold.at[slot], at, piece, read_packed(rcv1, slot, piece, ONE))
             send_packed(snd3, slot, piece, hold[slot, pl.ds(at, size)], TWO)
             packed_copy(2, slot, piece).start()
+
+    heard(2)
 
     for slot in (0, 1):
         half = (HALF, 0)[slot]
@@ -302,8 +332,8 @@
     all_counts = cnt[...] + cnt_in[0] + cnt_in[1] + cnt_in[2]
     weight = cnt[...] / jnp.sum(all_counts, axis=1, keepdims=True)
     adv, ratio = advantages[...], ratios[...]
-    active = jnp.where(adv >= 0.0, (ratio <= 1.0 + clip_eps).astype(F32), (ratio >= 1.0 - clip_eps).astype(F32))
-    policy = jnp.where(active > 0.5, -adv * ratio, jnp.zeros_like(ratio))
+    open_ = jnp.where(adv >= 0.0, (ratio <= 1.0 + clip_eps).astype(F32), (ratio >= 1.0 - clip_eps).astype(F32))
+    policy = jnp.where(open_ > 0.5, -adv * ratio, jnp.zeros_like(ratio))
     target = targets[...] - v * vocab_here
     target = jnp.where(target < vocab_here, target, -1)
     inverse = 1.0 / total
@@ -333,16 +363,19 @@
     gradient_copy(0, 1).start()
 
     chunk = width // 4
-    units = chunk // 16
+    active = lax.rem(z, 2) == core
+    sender = lax.rem(z, 2) != core
 
     def partial(sources):
         right_side = [g[r] for r in sources]
         right_side = right_side[0] if len(sources) == 1 else jnp.concatenate(right_side, axis=1)
-
+        deep = NZ // 8
         for i in range(4):
             value = jnp.dot(head_t[pl.ds(i * chunk, chunk)], right_side, preferred_element_type=F32)
             for j, r in enumerate(sources):
-                prod[r, pl.ds(i * units, units)] = value[:, j * 128 : (j + 1) * 128].reshape(units, 2, 8, 128)
+                prod[r, pl.ds(i * deep, deep)] = value[:, j * 128 : (j + 1) * 128].reshape(
+                    deep, 2, NX, 16, 128
+                )
         for r in sources:
             pair(r).start()
 
@@ -354,51 +387,62 @@
         return remote(xs.at[r, k], xs_in.at[r, k], x_send.at[sem], x_recv.at[sem], along_x(k))
 
     def z_copy(r, k):
-        sem = r * NZ + k
+        m = lax.rem(z // 2 + k, NZ // 2)
+        there = 2 * m + core
+        slot = lax.rem(z - there + NZ, NZ)
         return remote(
-            zs.at[r, lax.rem(z + k, NZ)], zs_in.at[r, k], z_send.at[sem], z_recv.at[sem], along_z(k)
+            zs.at[r, m], zs_in.at[r, slot], z_send.at[r * NZ + k], z_recv.at[r * NZ + slot],
+            (me, there * GROUP + xc),
         )
 
     def to_x(r):
         pair(r).wait_recv()
-        for k in range(NX):
+        for k in (*range(1, NX), 0):
             there = lax.rem(x + k, NX)
-            value = mid_sum(r, there)
+            value = prod[r, :, core, there] + prod_in[r, :, there]
             if k == 0:
                 mid[r] = value
             else:
                 xs[r, k] = value.reshape(NZ * 8, 128).astype(BF16)
                 x_copy(r, k).start()
 
-    def mid_sum(r, there):
-        return jnp.stack(
-            [prod[r, zz * NX + there, core] + prod_in[r, zz * NX + there] for zz in range(NZ)]
-        )
-
     def to_z(r):
         value = mid[r]
         for k in range(1, NX):
             x_copy(r, k).wait_recv()
-            value = value + xs_in[r, k].astype(F32).reshape(NZ, 8, 128)
-        zs[r] = value
+            value = value + xs_in[r, k].astype(F32).reshape(NZ // 2, 16, 128)
+        mid[r] = value
+        zs[r] = value.astype(BF16)
 
         def go(k, carry):
             z_copy(r, k).start()
             return carry
 
-        lax.fori_loop(1, NZ, go, 0)
+        lax.fori_loop(1, NZ // 2, go, 0)
+
+        @pl.when(sender)
+        def _():
+            z_copy(r, 0).start()
 
     def finish(r):
         def arrive(k, carry):
-            z_copy(r, k).wait_recv()
+            remote(
+                zs.at[r, 0], zs_in.at[r, k], z_send.at[r * NZ], z_recv.at[r * NZ + k],
+                (me, lax.rem(z + k, NZ) * GROUP + xc),
+            ).wait_recv()
             return carry
 
         lax.fori_loop(1, NZ, arrive, 0)
-        value = zs[r, z]
+        value = mid[r, z // 2]
         for k in range(1, NZ):
-            value = value + zs_in[r, k]
-        tokens = lax.rem(me + r, 4) * 128
-        total_h[:, pl.ds(pl.multiple_of(tokens, 128), 128)] = value
+            value = value + zs_in[r, k].astype(F32)
+        tokens = pl.ds(pl.multiple_of(lax.rem(me + r, 4) * 128, 128), 128)
+        total_h[0, :, tokens] = value[:8]
+        total_h[1, :, tokens] = value[8:]
+
+    last = remote(
+        total_h.at[1 - core], total_h.at[1 - core], f_sem.at[0], f_sem.at[1], sibling
+    )
 
     head_rows = ((0, 304), (304, 304), (608, 304), (912, vocab_here - 912))
 
@@ -407,41 +451,44 @@
         rows = pl.ds(at, size)
         left_side = jnp.concatenate([g[r, rows] for r in range(4)], axis=1)
         tokens = hid[...].reshape(4 * hid.shape[1], width)
-        head_o[rows] = jnp.dot(left_side, tokens, preferred_element_type=F32).astype(BF16)
-        head_copy(k).start()
-
-    def head_copy(k):
-        at, size = head_rows[k]
-        return pltpu.make_async_copy(head_o.at[pl.ds(at, size)], out_head.at[pl.ds(at, size)], o_sem.at[k])
+        out_head[rows] = jnp.dot(left_side, tokens, preferred_element_type=F32).astype(BF16)
 
     partial((0,))
-    to_x(0)
     gradient_copy(0, 0).wait_recv()
     gradient_copy(0, 2).start()
     gradient_copy(1, 0).wait_recv()
     gradient_copy(1, 2).start()
+    to_x(0)
     to_z(0)
     gradient_copy(0, 1).wait_recv()
     gradient_copy(1, 1).wait_recv()
     partial((1, 3))
     to_x(1)
     to_x(3)
-    to_z(1)
-    to_z(3)
     gradient_copy(0, 2).wait_recv()
     gradient_copy(1, 2).wait_recv()
     partial((2,))
     head_gradient(0)
     to_x(2)
+    to_z(1)
+    to_z(3)
     head_gradient(1)
     head_gradient(2)
     to_z(2)
     head_gradient(3)
-    finish(0)
-    finish(1)
-    finish(3)
-    finish(2)
-    out_hidden[...] = total_h[...].astype(BF16)
+
+    @pl.when(active)
+    def _():
+        for r in (0, 1, 3, 2):
+            finish(r)
+        last.start()
+        last.wait_send()
+
+    @pl.when(sender)
+    def _():
+        last.wait_recv()
+
+    out_hidden[...] = total_h[core].astype(BF16)
 
     for copy in (h_right, h_left, h_far, h_on, share[1], share[2], share[3]):
         copy.wait_send()
@@ -461,9 +508,11 @@
             z_copy(r, k).wait_send()
             return carry
 
-        lax.fori_loop(1, NZ, left_z, 0)
-    for k in range(4):
-        head_copy(k).wait()
+        lax.fori_loop(1, NZ // 2, left_z, 0)
+
+        @pl.when(sender)
+        def _():
+            z_copy(r, 0).wait_send()
 
 
 def local(devices, hidden, head, frozen, norms, advantages, ratios, targets, counted):
@@ -472,12 +521,10 @@
     vocab_here = head.shape[1]
     NZ = devices // (2 * NX)
     GROUP = 2 * NX
-    units = width // 16
     packed = pltpu.VMEM((2, HALF // 4 * 3, tokens), jnp.int32)
     dma = pltpu.SemaphoreType.DMA
     row = [a.reshape(1, tokens) for a in (norms, advantages, ratios, targets, counted)]
     vmem = pl.BlockSpec(memory_space=pltpu.VMEM)
-    anywhere = pl.BlockSpec(memory_space=pl.ANY)
     out = pl.pallas_call(
         functools.partial(kernel, devices),
         out_shape=(
@@ -485,9 +532,14 @@
             jax.ShapeDtypeStruct((vocab_here, width), BF16),
             jax.ShapeDtypeStruct((1, tokens), F32),
         ),
-        in_specs=[anywhere] * 3 + [vmem] * 5,
-        out_specs=(vmem, anywhere, vmem),
+        in_specs=[pl.BlockSpec(memory_space=pltpu.HBM)] * 8,
+        out_specs=(vmem, vmem, vmem),
         scratch_shapes=[
+            pltpu.VMEM((1, tokens), F32),
+            pltpu.VMEM((1, tokens), F32),
+            pltpu.VMEM((1, tokens), F32),
+            pltpu.VMEM((1, tokens), jnp.int32),
+            pltpu.VMEM((1, tokens), jnp.int32),
             pltpu.VMEM((vocab_here, width), BF16),
             pltpu.VMEM((width, DEEP), BF16),
             pltpu.VMEM((128, width), BF16),
@@ -505,16 +557,15 @@
             pltpu.VMEM((4, tokens), F32),
             pltpu.VMEM((NZ, 4, tokens), F32),
             pltpu.VMEM((4, DEEP, tokens), BF16),
-            pltpu.VMEM((4, units, 2, 8, tokens), F32),
-            pltpu.VMEM((4, units, 8, tokens), F32),
-            pltpu.VMEM((4, NZ, 8, tokens), F32),
+            pltpu.VMEM((4, NZ // 2, 2, NX, 16, tokens), F32),
+            pltpu.VMEM((4, NZ // 2, NX, 16, tokens), F32),
+            pltpu.VMEM((4, NZ // 2, 16, tokens), F32),
             pltpu.VMEM((4, NX, NZ * 8, tokens), BF16),
             pltpu.VMEM((4, NX, NZ * 8, tokens), BF16),
-            pltpu.VMEM((4, NZ, 8, tokens), F32),
-            pltpu.VMEM((4, NZ, 8, tokens), F32),
-            pltpu.VMEM((8, 4 * tokens), F32),
-            pltpu.VMEM((vocab_here, width), BF16),
-            dma((3,)),
+            pltpu.VMEM((4, NZ // 2, 16, tokens), BF16),
+            pltpu.VMEM((4, NZ, 16, tokens), BF16),
+            pltpu.VMEM((2, 8, 4 * tokens), F32),
+            dma((8,)),
             dma((4,)), dma((4,)),
             dma((4,)), dma((4,)),
             dma((12,)), dma((12,)),
@@ -525,12 +576,13 @@
             dma((4,)), dma((4,)),
             dma((4 * NX,)), dma((4 * NX,)),
             dma((4 * NZ,)), dma((4 * NZ,)),
-            dma((4,)),
+            dma((2,)),
+            pltpu.SemaphoreType.REGULAR((3,)),
         ],
         compiler_params=pltpu.CompilerParams(
             collective_id=0, has_side_effects=True, vmem_limit_bytes=48 * 1024 * 1024
         ),
-    )(hidden, head.T, frozen.T, *row)
+    )(*(pltpu.with_memory_space_constraint(a, pltpu.HBM) for a in (hidden, head.T, frozen.T, *row)))
     return out[0].T, out[1].T, out[2].reshape(tokens)
 
 

time: 96.9 us -> 85.6 us (0.88)
  local copies, waits for them, and re-layouts: 8 us -> 2.54 us
  Pallas kernels: 87.2 us -> 82.3 us
    unnamed x17 -> x3, local copies, waits for them, and re-layouts: 8 us -> 2.54 us
    pallas_call x1, Pallas kernels: 87.2 us -> 82.3 us  [local(): pl.pallas_call(functools.partial(kernel, devices), out_shape=(jax.ShapeDt...]
where the time goes in v2:
time: 85.6 us; the launch traced here: 85.4 us
  Pallas kernels  82.3 us (96%)
  local copies, waits for them, and re-layouts  2.54 us (3%)
    pallas_call x1, Pallas kernels, local(): pl.pallas_call(functools.partial(kernel, devices), out_shape=(jax.ShapeDt...  82.3 us
    unnamed x3, local copies, waits for them, and re-layouts  2.54 us

profile of v2, /device:TPU:1, one launch (start us, length us, event | category | flops | bytes accessed | tf_op | source)
XLA Modules:
  0.0 85.4 jit_solution(684582648712971189)
XLA Ops:
  0.6 82.3 %shard_map.103 = (bf16[8,512]{1,0:T(8,128)(2,1)S(1)}, bf16[1187,1024]{1,0:T(8,128)(2,1)S(1)}, f32[1,128]{1,0:T(1,128)S(1)}) custom-call(bf16[128,4096]{1,0:T(8,128)(2,1)} %hidden.1, bf16[1187,1024]{1,0:T(8,128)(2,1)} %bitcast.13, bf16[1187,128]{1,0:T(8,128)(2,1)} %bitcast.14, f32[1,128]{1,0:T(1,128)} %bitcast.15, f32[1,128]{1,0:T(1,128)} %bitcast.16, ...), custom_call_target="tpu_custom_call" | custom-call | tf_op jit(solution)/shard_map/pallas_call | solution.py:528
  82.9 0.6 copy.14
  83.5 1.4 %copy.15 = bf16[1024,1187]{0,1:T(8,128)(2,1)} copy(bf16[1024,1187]{0,1:T(8,128)(2,1)S(1)} %bitcast.10) | data formatting | bytes 4861952
  84.9 0.5 copy.16

commit v3 on v2

--- a/solution.py
+++ b/solution.py
@@ -13,7 +13,8 @@
 NX = 4
 HALF = 608
 PIECES = ((0, 320), (320, 288))
-SENT = (608, 592)
+EARLY = 320
+LATE = (288, 272)
 ROWS = 2 * HALF
 DEEP = 1280
 ONE = 512.0
@@ -50,10 +51,10 @@
     norms, advantages, ratios, targets, counted, head_v, head_t, tail, frozen_v, frozen_f, hid, via, logits, hold,
     snd2, snd1, snd3, rcv2, rcv1, rcv3,
     cnt, cnt_in, st1, st1_in, st2, st2_in,
-    g, prod, prod_in, mid, xs, xs_in, zs, zs_in, total_h,
+    eu, terms, terms_in, g, prod, prod_in, mid, xs, xs_in, zs, zs_in, total_h,
     load_sem, h_send, h_recv, sh_send, sh_recv, r_send, r_recv,
     c_send, c_recv, s1_send, s1_recv, s2_send, s2_recv,
-    g_send, g_recv, a_send, a_recv, x_send, x_recv, z_send, z_recv, f_sem, hello,
+    e_send, e_recv, t_send, t_recv, g_send, g_recv, a_send, a_recv, x_send, x_recv, z_send, z_recv, f_sem, hello,
 ):
     NZ = devices // (2 * NX)
     GROUP = 2 * NX
@@ -108,7 +109,7 @@
     barrier = pltpu.get_barrier_semaphore()
 
     near_y = [(lax.rem(me + k, 4), v) for k in (1, 3)]
-    near_x = [along_x(k) for k in (1, NX - 1)]
+    near_x = [along_x(k) for k in (1, NX - 1)] if NX > 1 else []
 
     def near_z(k):
         return [along_z(k), along_z(NZ - k)]
@@ -134,9 +135,9 @@
     h_left = remote(hidden.at[mine, lanes(left)], hid.at[1, mine], h_send.at[1], h_recv.at[1], (left, v))
     h_far = remote(hidden.at[mine, lanes(far)], via, h_send.at[2], h_recv.at[2], onward)
     h_on = remote(via, hid.at[2, mine], h_send.at[3], h_recv.at[3], onward)
-    h_far.start()
     h_right.start()
     h_left.start()
+    h_far.start()
     counts = [
         remote(cnt, cnt_in.at[k - 1], c_send.at[k - 1], c_recv.at[k - 1], (lax.rem(me + k, 4), v))
         for k in (1, 2, 3)
@@ -187,12 +188,12 @@
             ((right, left)[slot], v),
         )
 
-    h_far.wait_recv()
-    h_on.start()
     h_left.wait_recv()
     share[1].start()
     h_right.wait_recv()
     share[3].start()
+    h_far.wait_recv()
+    h_on.start()
 
     heard(0)
     tell(1)
@@ -293,7 +294,7 @@
         total += jnp.sum(shifted, axis=0, keepdims=True)
         cross += jnp.sum(shifted * (logits[piece] - frozen_f[piece]), axis=0, keepdims=True)
 
-    def exchange(top, total, cross, out, into, send, recv, to, count):
+    def exchange(top, total, cross, out, into, send, recv, to, count, meanwhile):
         out[0:1] = top
         out[1:2] = total
         out[2:3] = cross
@@ -308,6 +309,7 @@
             return carry
 
         lax.fori_loop(1, count, go, 0)
+        meanwhile()
         lax.fori_loop(1, count, arrive, 0)
         best = top
         for k in range(1, count):
@@ -320,10 +322,45 @@
             all_cross += into[k, 2:3] * scale
         return best, all_total, all_cross
 
+    top_here = top
+    centre = cross / total
+
+    def early_copy(slot, kind):
+        device = ((right, left)[slot], v)
+        half = (slot, 1 - slot, slot)[kind]
+        source = ((0, 0, 3), (0, 0, 1))[slot][kind]
+        into = ((3, 3, 2), (1, 1, 2))[slot][kind]
+        sem = slot * 3 + kind
+        return remote(
+            eu.at[source, half], eu.at[into, half], e_send.at[sem], e_recv.at[sem], device
+        )
+
+    def send_early():
+        for half in (0, 1):
+            for k in (0, 1):
+                at = k * (EARLY // 2)
+                piece = pl.ds(half * HALF + at, EARLY // 2)
+                value = logits[piece]
+                shifted = jnp.exp(value - top_here)
+                eu[0, half, pl.ds(at, EARLY // 2)] = shifted.astype(BF16)
+                eu[0, half, pl.ds(EARLY + at, EARLY // 2)] = (
+                    shifted * (value - frozen_f[piece] - centre)
+                ).astype(BF16)
+            early_copy(half, 0).start()
+        early_copy(1, 1).start()
+        early_copy(0, 1).start()
+
+    def pass_early():
+        for slot in (0, 1):
+            early_copy(slot, 0).wait_recv()
+            early_copy(slot, 2).start()
+
     top, total, cross = exchange(
-        top, total, cross, st1, st1_in, s1_send, s1_recv, in_group, GROUP
+        top, total, cross, st1, st1_in, s1_send, s1_recv, in_group, GROUP, send_early
     )
-    top, total, cross = exchange(top, total, cross, st2, st2_in, s2_send, s2_recv, along_z, NZ)
+    top, total, cross = exchange(
+        top, total, cross, st2, st2_in, s2_send, s2_recv, along_z, NZ, pass_early
+    )
     mean = cross / total
     out_div[...] = mean - top - jnp.log(total) + norms[...]
 
@@ -338,29 +375,57 @@
     target = jnp.where(target < vocab_here, target, -1)
     inverse = 1.0 / total
     hits = weight * policy
+    terms[0:1] = weight * jnp.exp(top_here - top) * inverse
+    terms[1:2] = penalty * (mean - centre) + policy
+    terms[2:3] = hits
+    terms[3:4] = target.astype(F32)
+    tell_terms = [
+        remote(terms, terms_in.at[k - 1], t_send.at[k - 1], t_recv.at[k - 1], (lax.rem(me + k, 4), v))
+        for k in (1, 2, 3)
+    ]
+    for copy in tell_terms:
+        copy.start()
 
     def gradient_copy(slot, kind):
         device = ((right, left)[slot], v)
         half = (slot, 1 - slot, slot)[kind]
-        rows = pl.ds(half * HALF, SENT[half])
+        rows = pl.ds(half * HALF + EARLY, LATE[half])
         source = ((0, 0, 3), (0, 0, 1))[slot][kind]
         into = ((3, 3, 2), (1, 1, 2))[slot][kind]
         sem = slot * 3 + kind
         return remote(g.at[source, rows], g.at[into, rows], g_send.at[sem], g_recv.at[sem], device)
 
-    for k in range(4):
-        piece = pl.ds(k * step, step)
+    def own_gradient(at, size):
+        piece = pl.ds(at, size)
         value = logits[piece]
         chance = jnp.exp(value - top) * inverse
-        rows = k * step + lax.broadcasted_iota(jnp.int32, value.shape, 0)
+        rows = at + lax.broadcasted_iota(jnp.int32, value.shape, 0)
         grad = weight * (penalty * chance * (value - frozen_f[piece] - mean) - policy * chance)
         grad = jnp.where(rows == target, grad + hits, grad)
         g[0, piece] = grad.astype(BF16)
-        if k == 1:
-            gradient_copy(0, 0).start()
-            gradient_copy(1, 1).start()
+
+    own_gradient(EARLY, HALF - EARLY)
+    gradient_copy(0, 0).start()
+    own_gradient(HALF + EARLY, HALF - EARLY)
     gradient_copy(1, 0).start()
+    gradient_copy(1, 1).start()
     gradient_copy(0, 1).start()
+    own_gradient(0, EARLY)
+    own_gradient(HALF, EARLY)
+
+    def early_gradient(r):
+        alpha, kappa, hit, there = (terms_in[3 - r, k : k + 1] for k in range(4))
+        there = there.astype(jnp.int32)
+        for half in (0, 1):
+            for k in (0, 1):
+                at = k * (EARLY // 2)
+                shifted = eu[r, half, pl.ds(at, EARLY // 2)].astype(F32)
+                moved = eu[r, half, pl.ds(EARLY + at, EARLY // 2)].astype(F32)
+                grad = alpha * (penalty * moved - kappa * shifted)
+                at = half * HALF + at
+                rows = at + lax.broadcasted_iota(jnp.int32, grad.shape, 0)
+                grad = jnp.where(rows == there, grad + hit, grad)
+                g[r, pl.ds(at, EARLY // 2)] = grad.astype(BF16)
 
     chunk = width // 4
     active = lax.rem(z, 2) == core
@@ -454,15 +519,24 @@
         out_head[rows] = jnp.dot(left_side, tokens, preferred_element_type=F32).astype(BF16)
 
     partial((0,))
+    for copy in tell_terms:
+        copy.wait_recv()
     gradient_copy(0, 0).wait_recv()
     gradient_copy(0, 2).start()
     gradient_copy(1, 0).wait_recv()
     gradient_copy(1, 2).start()
     to_x(0)
-    to_z(0)
+    for slot in (0, 1):
+        early_copy(slot, 1).wait_recv()
+    early_gradient(1)
+    early_gradient(3)
     gradient_copy(0, 1).wait_recv()
     gradient_copy(1, 1).wait_recv()
     partial((1, 3))
+    to_z(0)
+    for slot in (0, 1):
+        early_copy(slot, 2).wait_recv()
+    early_gradient(2)
     to_x(1)
     to_x(3)
     gradient_copy(0, 2).wait_recv()
@@ -499,6 +573,9 @@
     for slot in (0, 1):
         for kind in range(3):
             gradient_copy(slot, kind).wait_send()
+            early_copy(slot, kind).wait_send()
+    for copy in tell_terms:
+        copy.wait_send()
     for r in range(4):
         pair(r).wait_send()
         for k in range(1, NX):
@@ -556,6 +633,9 @@
             pltpu.VMEM((GROUP, 4, tokens), F32),
             pltpu.VMEM((4, tokens), F32),
             pltpu.VMEM((NZ, 4, tokens), F32),
+            pltpu.VMEM((4, 2, 2 * EARLY, tokens), BF16),
+            pltpu.VMEM((4, tokens), F32),
+            pltpu.VMEM((3, 4, tokens), F32),
             pltpu.VMEM((4, DEEP, tokens), BF16),
             pltpu.VMEM((4, NZ // 2, 2, NX, 16, tokens), F32),
             pltpu.VMEM((4, NZ // 2, NX, 16, tokens), F32),
@@ -573,6 +653,8 @@
             dma((GROUP,)), dma((GROUP,)),
             dma((NZ,)), dma((NZ,)),
             dma((6,)), dma((6,)),
+            dma((3,)), dma((3,)),
+            dma((6,)), dma((6,)),
             dma((4,)), dma((4,)),
             dma((4 * NX,)), dma((4 * NX,)),
             dma((4 * NZ,)), dma((4 * NZ,)),

time: 85.6 us -> 80.6 us (0.942)
  Pallas kernels: 82.3 us -> 77.3 us
    pallas_call x1, Pallas kernels: 82.3 us -> 77.3 us  [local(): pl.pallas_call(functools.partial(kernel, devices), out_shape=(jax.ShapeDt...]
where the time goes in v3:
time: 80.6 us; the launch traced here: 80.5 us
  Pallas kernels  77.3 us (96%)
  local copies, waits for them, and re-layouts  2.54 us (3%)
    pallas_call x1, Pallas kernels, local(): pl.pallas_call(functools.partial(kernel, devices), out_shape=(jax.ShapeDt...  77.3 us
    unnamed x3, local copies, waits for them, and re-layouts  2.54 us

profile of v3, /device:TPU:1, one launch (start us, length us, event | category | flops | bytes accessed | tf_op | source)
XLA Modules:
  0.0 80.5 jit_solution(2711070943491347669)
XLA Ops:
  0.6 77.3 %shard_map.103 = (bf16[8,512]{1,0:T(8,128)(2,1)S(1)}, bf16[1187,1024]{1,0:T(8,128)(2,1)S(1)}, f32[1,128]{1,0:T(1,128)S(1)}) custom-call(bf16[128,4096]{1,0:T(8,128)(2,1)} %hidden.1, bf16[1187,1024]{1,0:T(8,128)(2,1)} %bitcast.13, bf16[1187,128]{1,0:T(8,128)(2,1)} %bitcast.14, f32[1,128]{1,0:T(1,128)} %bitcast.15, f32[1,128]{1,0:T(1,128)} %bitcast.16, ...), custom_call_target="tpu_custom_call" | custom-call | tf_op jit(solution)/shard_map/pallas_call | solution.py:605
  78.0 0.6 copy.14
  78.6 1.4 %copy.15 = bf16[1024,1187]{0,1:T(8,128)(2,1)} copy(bf16[1024,1187]{0,1:T(8,128)(2,1)S(1)} %bitcast.10) | data formatting | bytes 4861952
  80.0 0.5 copy.16

commit v4 on v3

--- a/solution.py
+++ b/solution.py
@@ -294,13 +294,17 @@
         total += jnp.sum(shifted, axis=0, keepdims=True)
         cross += jnp.sum(shifted * (logits[piece] - frozen_f[piece]), axis=0, keepdims=True)
 
+    def far_first(i, count):
+        return count // 2 + (1 - 2 * lax.rem(i, 2)) * ((i + 1) // 2)
+
     def exchange(top, total, cross, out, into, send, recv, to, count, meanwhile):
         out[0:1] = top
         out[1:2] = total
         out[2:3] = cross
         out[3:4] = cross
 
-        def go(k, carry):
+        def go(i, carry):
+            k = far_first(i, count)
             remote(out, into.at[k], send.at[k], recv.at[k], to(k)).start()
             return carry
 
@@ -308,7 +312,7 @@
             remote(out, into.at[k], send.at[k], recv.at[k], to(k)).wait()
             return carry
 
-        lax.fori_loop(1, count, go, 0)
+        lax.fori_loop(0, count - 1, go, 0)
         meanwhile()
         lax.fori_loop(1, count, arrive, 0)
         best = top
@@ -462,7 +466,7 @@
 
     def to_x(r):
         pair(r).wait_recv()
-        for k in (*range(1, NX), 0):
+        for k in (*sorted(range(1, NX), key=lambda k: -min(k, NX - k)), 0):
             there = lax.rem(x + k, NX)
             value = prod[r, :, core, there] + prod_in[r, :, there]
             if k == 0:
@@ -479,11 +483,11 @@
         mid[r] = value
         zs[r] = value.astype(BF16)
 
-        def go(k, carry):
-            z_copy(r, k).start()
+        def go(i, carry):
+            z_copy(r, far_first(i, NZ // 2)).start()
             return carry
 
-        lax.fori_loop(1, NZ // 2, go, 0)
+        lax.fori_loop(0, NZ // 2 - 1, go, 0)
 
         @pl.when(sender)
         def _():

time: 80.6 us -> 80.1 us (level)
  no operation moved by 1% of the time
where the time goes in v4:
time: 80.1 us; the launch traced here: 79.9 us
  Pallas kernels  76.7 us (96%)
  local copies, waits for them, and re-layouts  2.54 us (3%)
    pallas_call x1, Pallas kernels, local(): pl.pallas_call(functools.partial(kernel, devices), out_shape=(jax.ShapeDt...  76.7 us
    unnamed x3, local copies, waits for them, and re-layouts  2.54 us

profile of v4, /device:TPU:1, one launch (start us, length us, event | category | flops | bytes accessed | tf_op | source)
XLA Modules:
  0.0 79.9 jit_solution(9889378046492607080)
XLA Ops:
  0.6 76.7 %shard_map.103 = (bf16[8,512]{1,0:T(8,128)(2,1)S(1)}, bf16[1187,1024]{1,0:T(8,128)(2,1)S(1)}, f32[1,128]{1,0:T(1,128)S(1)}) custom-call(bf16[128,4096]{1,0:T(8,128)(2,1)} %hidden.1, bf16[1187,1024]{1,0:T(8,128)(2,1)} %bitcast.13, bf16[1187,128]{1,0:T(8,128)(2,1)} %bitcast.14, f32[1,128]{1,0:T(1,128)} %bitcast.15, f32[1,128]{1,0:T(1,128)} %bitcast.16, ...), custom_call_target="tpu_custom_call" | custom-call | tf_op jit(solution)/shard_map/pallas_call | solution.py:609
  77.4 0.6 copy.14
  78.0 1.4 %copy.15 = bf16[1024,1187]{0,1:T(8,128)(2,1)} copy(bf16[1024,1187]{0,1:T(8,128)(2,1)S(1)} %bitcast.10) | data formatting | bytes 4861952
  79.4 0.5 copy.16

commit v5 on v4

--- a/solution.py
+++ b/solution.py
@@ -12,7 +12,7 @@
 
 NX = 4
 HALF = 608
-PIECES = ((0, 320), (320, 288))
+PIECES = ((0, 352), (352, 256))
 EARLY = 320
 LATE = (288, 272)
 ROWS = 2 * HALF

time: 80.1 us -> 80.1 us (level)
  no operation moved by 1% of the time
where the time goes in v5:
time: 80.1 us; the launch traced here: 80 us
  Pallas kernels  76.8 us (96%)
  local copies, waits for them, and re-layouts  2.54 us (3%)
    pallas_call x1, Pallas kernels, local(): pl.pallas_call(functools.partial(kernel, devices), out_shape=(jax.ShapeDt...  76.8 us
    unnamed x3, local copies, waits for them, and re-layouts  2.54 us

profile of v5, /device:TPU:1, one launch (start us, length us, event | category | flops | bytes accessed | tf_op | source)
XLA Modules:
  0.0 80.0 jit_solution(5322855004898778411)
XLA Ops:
  0.6 76.8 %shard_map.103 = (bf16[8,512]{1,0:T(8,128)(2,1)S(1)}, bf16[1187,1024]{1,0:T(8,128)(2,1)S(1)}, f32[1,128]{1,0:T(1,128)S(1)}) custom-call(bf16[128,4096]{1,0:T(8,128)(2,1)} %hidden.1, bf16[1187,1024]{1,0:T(8,128)(2,1)} %bitcast.13, bf16[1187,128]{1,0:T(8,128)(2,1)} %bitcast.14, f32[1,128]{1,0:T(1,128)} %bitcast.15, f32[1,128]{1,0:T(1,128)} %bitcast.16, ...), custom_call_target="tpu_custom_call" | custom-call | tf_op jit(solution)/shard_map/pallas_call | solution.py:609
  77.4 0.6 copy.14
  78.0 1.4 %copy.15 = bf16[1024,1187]{0,1:T(8,128)(2,1)} copy(bf16[1024,1187]{0,1:T(8,128)(2,1)S(1)} %bitcast.10) | data formatting | bytes 4861952
  79.5 0.5 copy.16
